TPU v7x, 32 devices: a whole 2x2x4 slice. The times are simulated.
32 devices in a mesh: cfg: 2 (over x), req: 4 (over z), seq: 4 (over y, core).
Axes of the slice: x: 2, y: 2, z: 4, core: 2. Of those that a mesh axis runs over, the one named last changes fastest.
Arguments:
- img_state: bfloat16 [2, 8, 1024, 1536], P('cfg', 'req', 'seq'), may hold values from -6 to 6
- txt_state: bfloat16 [2, 8, 192, 1536], P('cfg', 'req', 'seq'), may hold values from -6 to 6
- cond_vec: float32 [2, 8, 1536], P('cfg'), may hold values from -6 to 6
- text_len: int32 [2, 8], P('cfg', 'req'), may hold values from 38 to 154, as said below
- latent: float32 [8, 1024, 64], P('req', 'seq', 'cfg'), may hold values from -6 to 6
- w_mod: bfloat16 [15360, 1536], P(('req', 'seq')), may hold values from -0.15625 to 0.15625
- w_qkv_img: bfloat16 [3, 1536, 1536], P(None, 'seq')
- w_qkv_txt: bfloat16 [3, 1536, 1536], P(None, 'seq')
- w_attn_out: bfloat16 [1536, 1536], P('seq'), may hold values from -2 to 2
- w_up: bfloat16 [6144, 1536], P(('cfg', 'req', 'seq')), may hold values from -0.15625 to 0.15625
- w_down: bfloat16 [6144, 1536], P(('cfg', 'req', 'seq')), may hold values from -0.078125 to 0.078125
- w_final: bfloat16 [1536, 64], replicated, may hold values from -0.078125 to 0.078125
Outputs:
- velocity: float32 [8, 1024, 64], P('req', 'seq', 'cfg')
- latent_next: float32 [8, 1024, 64], P('req', 'seq', 'cfg')
Inputs may be any that keep to these rules, and one draw needn't show every extreme that they name: Text slot t of prompt p in branch c is live when t < text_len[c, p]; every draw has a length equal to 154.
All inputs are finite; a program needn't handle non-finite values.
Results may differ from a plain program's by a relative error of at most 0.02.
Values may be sent and summed in bfloat16 or wider, within the bound.
A program may use at most 128 MiB of HBM per device.

v0:
```python
import jax
import jax.numpy as jnp
from jax import lax
from jax.sharding import PartitionSpec as P

HEAD = 64


def partner_2(shard, axis, apart):
    return lax.ppermute(shard, axis, [(i, i ^ 1 << apart) for i in range(lax.axis_size(axis))])


def layer_norm(value):
    mean = jnp.mean(value, axis=-1, keepdims=True)
    centered = value - mean
    spread = jnp.mean(centered * centered, axis=-1, keepdims=True)
    return centered * lax.rsqrt(spread + 1e-06)


def mlp_term(rows_in, up_block, down_block):
    inner = lax.dot_general(
        rows_in, up_block, (((1,), (1,)), ((), ())), preferred_element_type=jnp.float32
    )
    hidden = jax.nn.gelu(inner, approximate=True).astype(jnp.bfloat16)
    return jnp.dot(hidden, down_block, preferred_element_type=jnp.float32)


def local(
    img_state,
    txt_state,
    cond_vec,
    text_len,
    latent,
    w_mod,
    w_qkv_img,
    w_qkv_txt,
    w_attn_out,
    w_up,
    w_down,
    w_final,
):
    prompts_dev = img_state.shape[1]
    img_rows = img_state.shape[2]
    width = img_state.shape[3]
    cond_act = jax.nn.silu(cond_vec[0]).astype(jnp.bfloat16)
    mod_part = lax.dot_general(
        cond_act, w_mod, (((1,), (1,)), ((), ())), preferred_element_type=jnp.float32
    )
    mod_all = lax.all_gather(mod_part, ("req", "seq"), axis=1, tiled=True)
    mine = lax.dynamic_slice_in_dim(mod_all, lax.axis_index("req") * prompts_dev, prompts_dev, 0)
    parts = mine.reshape(prompts_dev, 10, 1, width)
    resid = img_state[0].astype(jnp.float32)
    a_img = (layer_norm(resid) * (1.0 + parts[:, 1]) + parts[:, 0]).astype(jnp.bfloat16)
    a_txt = (
        layer_norm(txt_state[0].astype(jnp.float32)) * (1.0 + parts[:, 7]) + parts[:, 6]
    ).astype(jnp.bfloat16)
    full_img, full_txt = (
        lax.all_gather(a_img, "seq", axis=1, tiled=True),
        lax.all_gather(a_txt, "seq", axis=1, tiled=True),
    )
    proj_img = jnp.einsum(
        "pnd,jed->jpne", full_img, w_qkv_img, preferred_element_type=jnp.float32
    ).astype(jnp.bfloat16)
    proj_txt = jnp.einsum(
        "pnd,jed->jpne", full_txt, w_qkv_txt, preferred_element_type=jnp.float32
    ).astype(jnp.bfloat16)
    total_img = full_img.shape[1]
    local_width = w_qkv_img.shape[1]
    heads_local = local_width // HEAD
    key_heads = jnp.concatenate([proj_img[1], proj_txt[1]], axis=1).reshape(
        prompts_dev, -1, heads_local, HEAD
    )
    value_heads = jnp.concatenate([proj_img[2], proj_txt[2]], axis=1).reshape(
        prompts_dev, -1, heads_local, HEAD
    )
    live = jnp.arange(key_heads.shape[1])[None, :] < (total_img + text_len[0])[:, None]
    block = min(512, total_img)
    queries = proj_img[0].reshape(prompts_dev, total_img // block, block, heads_local, HEAD)

    def attend(query):
        scores = jnp.einsum(
            "pqhe,pkhe->phqk", query, key_heads, preferred_element_type=jnp.float32
        ) * HEAD ** (-0.5)
        scores = jnp.where(live[:, None, None, :], scores, -1e30)
        probs = jax.nn.softmax(scores, axis=-1).astype(jnp.bfloat16)
        return jnp.einsum(
            "phqk,pkhe->pqhe", probs, value_heads, preferred_element_type=jnp.float32
        ).astype(jnp.bfloat16)

    attended = lax.map(attend, jnp.moveaxis(queries, 1, 0))
    attended = jnp.moveaxis(attended, 0, 1).reshape(prompts_dev, total_img, local_width)
    proj = jnp.swapaxes(
        lax.psum_scatter(
            jnp.einsum(
                "pnh,hd->npd", attended, w_attn_out, preferred_element_type=jnp.float32
            ).astype(jnp.bfloat16),
            "seq",
            scatter_dimension=0,
            tiled=True,
        ).astype(jnp.float32),
        0,
        1,
    )
    resid_one = (resid + parts[:, 2] * proj).astype(jnp.bfloat16)
    normed = (layer_norm(resid_one.astype(jnp.float32)) * (1.0 + parts[:, 4]) + parts[:, 3]).astype(
        jnp.bfloat16
    )
    own_rows = normed.reshape(prompts_dev * img_rows, width)
    both = lax.all_gather(own_rows, "cfg", axis=0, tiled=True)
    partial_out = mlp_term(
        both,
        lax.all_gather(w_up, ("req", "seq"), axis=0, tiled=True),
        lax.all_gather(w_down, ("req", "seq"), axis=0, tiled=True),
    )
    mlp_out = lax.psum_scatter(
        partial_out.astype(jnp.bfloat16), "cfg", scatter_dimension=0, tiled=True
    ).astype(jnp.float32)
    mlp_out = mlp_out.reshape(prompts_dev, img_rows, width)
    resid_two = resid_one.astype(jnp.float32) + parts[:, 5] * mlp_out
    final_in = (layer_norm(resid_two) * (1.0 + parts[:, 9]) + parts[:, 8]).astype(jnp.bfloat16)
    branch_vel = jnp.einsum("pnd,dc->pnc", final_in, w_final, preferred_element_type=jnp.float32)
    half_width = latent.shape[2]
    branch_index = lax.axis_index("cfg")
    own_half = lax.dynamic_slice_in_dim(branch_vel, branch_index * half_width, half_width, 2)
    other_half = lax.dynamic_slice_in_dim(
        branch_vel, (1 - branch_index) * half_width, half_width, 2
    )
    partner = partner_2(other_half.astype(jnp.bfloat16), "cfg", 0).astype(other_half.dtype)
    first = branch_index == 0
    cond_vel = jnp.where(first, own_half, partner)
    uncond_vel = jnp.where(first, partner, own_half)
    velocity = uncond_vel + 4.5 * (cond_vel - uncond_vel)
    latent_next = latent - 0.04 * velocity
    return (velocity, latent_next)


def solution(mesh):
    placed = (
        P("cfg", "req", "seq", None),
        P("cfg", "req", "seq", None),
        P("cfg", None, None),
        P("cfg", "req"),
        P("req", "seq", "cfg"),
        P(("req", "seq"), None),
        P(None, "seq", None),
        P(None, "seq", None),
        P("seq", None),
        P(("cfg", "req", "seq"), None),
        P(("cfg", "req", "seq"), None),
        P(),
    )
    return jax.shard_map(
        local,
        mesh=mesh,
        in_specs=placed,
        out_specs=(P("req", "seq", "cfg"), P("req", "seq", "cfg")),
        check_vma=False,
    )
```

profile of v0, /device:TPU:8, one launch (start us, length us, event | category | flops | bytes accessed | tf_op | source)
XLA Modules:
  0.0 524.3 jit_solution(5238276709531494205)
XLA Ops:
  8.1 2.9 convolution_bitcast_fusion
  10.9 20.3 %all-gather = f32[16,960,8]{1,2,0:T(8,128)S(1)} all-gather(f32[1,960,8]{1,2,0:T(8,128)S(1)} %convolution_bitcast_fusion), channel_id=1, replica_groups=mesh['cfg'=2,'req'=4,'seq'=4] {'req','seq'}, dimensions={0}, use_global_device_ids=true | all-gather | bytes 522240 | tf_op jit(solution)/shard_map/all_gather | solution.py:49
  31.3 1.1 copy.23
  32.4 2.1 reshape.139
  34.4 1.7 dynamic-slice_bitcast_fusion
  36.2 1.7 reshape.131
  37.8 2.3 fusion.103
  40.1 1.1 convert_reduce_fusion.2
  41.2 1.2 fusion.77
  42.4 1.9 fusion.80
  44.4 0.0 all-gather.7.cloned.1.call-start
  44.5 1.8 convert_reduce_fusion.1
  46.3 2.0 fusion.55
  48.3 1.8 fusion.58
  50.1 0.0 reduce-scatter.3.cloned.1.call-start
  50.2 11.8 %all-gather.9.cloned.1.call-done = bf16[2,192,1536]{2,1,0:T(8,128)(2,1)} async-done(((bf16[2,48,1536]{2,1,0:T(8,128)(2,1)}), bf16[2,192,1536]{2,1,0:T(8,128)(2,1)}) %all-gather.9.cloned.1.call-update) | async-done | bytes 1179664 | tf_op jit(solution)/shard_map/all_gather | solution.py:59
  62.0 4.1 fusion.69
  66.1 0.9 fusion.102
  67.0 1.9 copy.26
  68.9 2.0 copy.25
  70.9 39.1 %all-gather.7.cloned.1.call-done = bf16[2,1024,1536]{2,1,0:T(8,128)(2,1)} async-done(((bf16[2,256,1536]{2,1,0:T(8,128)(2,1)}), bf16[2,1024,1536]{2,1,0:T(8,128)(2,1)}) %all-gather.7.cloned.1.call-update) | async-done | bytes 6291472 | tf_op jit(solution)/shard_map/all_gather | solution.py:58
  110.0 9.7 %convert_bitcast_fusion.1 = bf16[3,2,1024,384]{2,3,0,1:T(8,128)(2,1)S(1)} fusion(bf16[3,384,1536]{2,1,0:T(8,128)(2,1)S(1)} %copy-done, bf16[2,1024,1536]{2,1,0:T(8,128)(2,1)} %all-gather.7.cloned.1.call-done), kind=kOutput, calls=%fused_computation.40 | convolution fusion | flops 7250116608 | bytes 14548992 | tf_op jit(solution)/shard_map/pnd,jed->jpne/dot_general | solution.py:61
  119.7 1.7 fusion.101
  121.4 3.9 reshape_squeeze.3
  125.3 2.9 copy.53
  128.2 1.5 pad_maximum_fusion.1
  129.7 1.5 pad_maximum_fusion
  131.2 0.8 copy-done.6
  132.0 63.7 %while.11 = (s32[]{:T(128)}, bf16[2,2,512,6,64]{2,4,3,1,0:T(8,128)(2,1)}, bf16[2,2,512,6,64]{2,4,3,1,0:T(8,128)(2,1)}, bf16[2,1216,6,64]{1,3,2,0:T(8,128)(2,1)},...) while((s32[]{:T(128)}, bf16[2,2,512,6,64]{2,4,3,1,0:T(8,128)(2,1)}, ...), condition=%wide.region_7.8_spmd.clone, body=%wide.region_4.7_spmd.clone.sunk | while | flops 1957826048 | bytes 77911432 | solution.py:90
  132.0 0.1 iota_compare_fusion.2
  132.1 18.4 %fusion.121 = (f32[2,6,512]{2,1,0:T(8,128)}, f32[2,6,512,1216]{2,3,1,0:T(8,128)}) fusion(pred[2,1216]{1,0:T(4,128)(4,1)S(1)} %iota_compare_fusion.2, bf16[2,1216,6,64]{1,3,2,0:T(8,128)(2,1)} %get-tuple-element.149, bf16[2,2,512,6,64]{2,4,3,1,0:T(8,128)(2,1)} %get-tuple-element.148, s32[]{:T(128)} %get-tuple-element.139), kind=kOutput, calls=%fused_computation.128.clone.1 | convolution fusion | flops 986186944 | bytes 32664448 | tf_op jit(solution)/shard_map/while/body/eval_jaxpr/sub | solution.py:85
  150.4 12.2 %fusion.122 = bf16[2,2,512,6,64]{2,4,3,1,0:T(8,128)(2,1)S(1)} fusion(bf16[2,2,512,6,64]{2,4,3,1,0:T(8,128)(2,1)S(1)} %copy-done.7, s32[]{:T(128)} %get-tuple-element.139, bf16[2,1216,6,64]{1,3,2,0:T(8,128)(2,1)S(1)} %get-tuple-element.150, f32[2,6,512,1216]{2,3,1,0:T(8,128)} %get-tuple-element.130, f32[2,6,512]{2,1,0:T(8,128)} %get-tuple-element.131), kind=kOutput, calls=%fused_computation.13.clone.1 | convolution fusion | flops 971636736 | bytes 32661508 | tf_op jit(solution)/shard_map/while/body/eval_jaxpr/phqk,pkhe->pqhe/dot_general | solution.py:86
  162.7 1.1 copy-done.8
  163.8 0.1 iota_compare_fusion.2
  163.9 18.4 %fusion.121 = (f32[2,6,512]{2,1,0:T(8,128)}, f32[2,6,512,1216]{2,3,1,0:T(8,128)}) fusion(pred[2,1216]{1,0:T(4,128)(4,1)S(1)} %iota_compare_fusion.2, bf16[2,1216,6,64]{1,3,2,0:T(8,128)(2,1)} %get-tuple-element.149, bf16[2,2,512,6,64]{2,4,3,1,0:T(8,128)(2,1)} %get-tuple-element.148, s32[]{:T(128)} %get-tuple-element.139), kind=kOutput, calls=%fused_computation.128.clone.1 | convolution fusion | flops 986186944 | bytes 32664448 | tf_op jit(solution)/shard_map/while/body/eval_jaxpr/sub | solution.py:85
  182.3 12.2 %fusion.122 = bf16[2,2,512,6,64]{2,4,3,1,0:T(8,128)(2,1)S(1)} fusion(bf16[2,2,512,6,64]{2,4,3,1,0:T(8,128)(2,1)S(1)} %copy-done.7, s32[]{:T(128)} %get-tuple-element.139, bf16[2,1216,6,64]{1,3,2,0:T(8,128)(2,1)S(1)} %get-tuple-element.150, f32[2,6,512,1216]{2,3,1,0:T(8,128)} %get-tuple-element.130, f32[2,6,512]{2,1,0:T(8,128)} %get-tuple-element.131), kind=kOutput, calls=%fused_computation.13.clone.1 | convolution fusion | flops 971636736 | bytes 32661508 | tf_op jit(solution)/shard_map/while/body/eval_jaxpr/phqk,pkhe->pqhe/dot_general | solution.py:86
  194.6 1.1 copy-done.8
  195.7 3.0 copy.27
  198.7 1.1 reshape.132
  199.9 6.7 %convert_bitcast_fusion = bf16[1024,2,1536]{2,0,1:T(8,128)(2,1)} fusion(bf16[2,1024,384]{1,2,0:T(8,128)(2,1)S(1)} %reshape.132, bf16[384,1536]{1,0:T(8,128)(2,1)} %param.22), kind=kOutput, calls=%fused_computation.35 | convolution fusion | flops 2419064832 | bytes 9043968 | tf_op jit(solution)/shard_map/pnh,hd->npd/dot_general | solution.py:94
  206.6 0.0 all-gather.13.cloned.1.call-start
  206.6 0.5 all-gather.13.cloned.1.call-update
  207.2 0.5 all-gather.15.cloned.1.call-update
  207.7 0.0 all-gather.11.cloned.1.call-start
  207.9 57.5 %reduce-scatter.3.cloned.1.call-done = bf16[256,2,1536]{2,0,1:T(8,128)(2,1)} async-done(((bf16[1024,2,1536]{2,0,1:T(8,128)(2,1)}), bf16[256,2,1536]{2,0,1:T(8,128)(2,1)}) %reduce-scatter.3.cloned.1.call-update) | async-done | bytes 1572880 | tf_op jit(solution)/shard_map/reduce_scatter | solution.py:93
  265.4 2.0 convert_reduce_fusion
  267.4 0.5 fusion.51
  268.0 1.8 fusion.54
  269.8 0.0 reduce-scatter.5.cloned.1.call-start
  269.9 36.2 %all-gather.13.cloned.1.call-done = bf16[3072,1536]{1,0:T(8,128)(2,1)} async-done(((bf16[192,1536]{1,0:T(8,128)(2,1)}), bf16[3072,1536]{1,0:T(8,128)(2,1)}) %all-gather.13.cloned.1.call-update) | async-done | bytes 9437200 | tf_op jit(solution)/shard_map/all_gather | solution.py:112
  306.1 81.6 %all-gather.15.cloned.1.call-done = bf16[3072,1536]{1,0:T(8,128)(2,1)} async-done(((bf16[192,1536]{1,0:T(8,128)(2,1)}), bf16[3072,1536]{1,0:T(8,128)(2,1)}) %all-gather.15.cloned.1.call-update) | async-done | bytes 9437200 | tf_op jit(solution)/shard_map/all_gather | solution.py:113
  387.6 45.1 %all-gather.11.cloned.1.call-done = bf16[1024,1536]{1,0:T(8,128)(2,1)} async-done(((bf16[512,1536]{1,0:T(8,128)(2,1)}), bf16[1024,1536]{1,0:T(8,128)(2,1)}) %all-gather.11.cloned.1.call-update) | async-done | bytes 3145744 | tf_op jit(solution)/shard_map/all_gather | solution.py:109
  432.8 28.0 %fusion.41 = bf16[1024,1536]{1,0:T(8,128)(2,1)} fusion(bf16[3072,1536]{1,0:T(8,128)(2,1)} %all-gather.15.cloned.1.call-done, bf16[1024,1536]{1,0:T(8,128)(2,1)} %all-gather.11.cloned.1.call-done, bf16[3072,1536]{1,0:T(8,128)(2,1)} %all-gather.13.cloned.1.call-done), kind=kOutput, calls=%fused_computation.45 | convolution fusion | flops 19357237248 | bytes 25165824 | tf_op jit(solution)/shard_map/dot_general | solution.py:25
  460.8 0.7 copy-done.12
  461.5 0.6 copy_bitcast_fusion.1
  462.1 42.1 %reduce-scatter.5.cloned.1.call-done = bf16[512,1536]{1,0:T(8,128)(2,1)} async-done(((bf16[1024,1536]{1,0:T(8,128)(2,1)}), bf16[512,1536]{1,0:T(8,128)(2,1)}) %reduce-scatter.5.cloned.1.call-update) | async-done | bytes 1572880 | tf_op jit(solution)/shard_map/reduce_scatter | solution.py:115
  504.2 2.1 fusion.64
  506.4 0.8 multiply_reduce_fusion
  507.2 2.7 fusion.65
  509.9 0.6 copy-done.11
  510.6 0.6 dynamic-slice_convert_fusion
  511.2 0.6 collective-permute-start
  511.8 3.7 collective-permute-done
  515.4 1.5 multiply_subtract_fusion
  (67 shorter events, 0.4 us)
Async XLA Ops:
  8.0 102.0 %copy-start = (bf16[3,384,1536]{2,1,0:T(8,128)(2,1)S(1)}, bf16[3,384,1536]{2,1,0:T(8,128)(2,1)}, u32[]{:S(2)}) copy-start(bf16[3,384,1536]{2,1,0:T(8,128)(2,1)} %param.20) | copy-start | bytes 10616836
  8.0 54.0 %all-gather.9.cloned.1.call-start = ((), (), s32[]{:S(2)}) async-start(), calls=%async_computation.3 | async-start | bytes 1474560 | tf_op jit(solution)/shard_map/all_gather | solution.py:59
  44.4 65.6 %all-gather.7.cloned.1.call-start = ((), (), s32[]{:S(2)}) async-start(), calls=%async_computation.2 | async-start | bytes 7864320 | tf_op jit(solution)/shard_map/all_gather | solution.py:58
  44.4 3.8 copy-start.18
  44.4 3.8 copy-start.3
  46.3 3.9 copy-start.22
  50.1 215.2 %reduce-scatter.3.cloned.1.call-start = ((), (), s32[]{:S(2)}) async-start(), calls=%async_computation.4 | async-start | bytes 7864320 | tf_op jit(solution)/shard_map/reduce_scatter | solution.py:93
  121.4 6.9 %copy-start.10 = (bf16[1,2,192,384]{2,3,1,0:T(8,128)(2,1)S(1)}, bf16[1,2,192,384]{2,3,1,0:T(8,128)(2,1)}, u32[]{:S(2)}) copy-start(bf16[1,2,192,384]{2,3,1,0:T(8,128)(2,1)} %copy.26) | copy-start | bytes 884740
  125.3 4.4 copy-start.9
  129.7 2.3 copy-start.6
  132.1 18.4 %copy-start.7 = (bf16[2,2,512,6,64]{2,4,3,1,0:T(8,128)(2,1)S(1)}, bf16[2,2,512,6,64]{2,4,3,1,0:T(8,128)(2,1)}, u32[]{:S(2)}) copy-start(bf16[2,2,512,6,64]{2,4,3,1,0:T(8,128)(2,1)} %get-tuple-element.140) | copy-start | bytes 4718596 | tf_op jit(solution)/shard_map/while
  162.7 1.1 copy-start.8
  163.9 18.4 %copy-start.7 = (bf16[2,2,512,6,64]{2,4,3,1,0:T(8,128)(2,1)S(1)}, bf16[2,2,512,6,64]{2,4,3,1,0:T(8,128)(2,1)}, u32[]{:S(2)}) copy-start(bf16[2,2,512,6,64]{2,4,3,1,0:T(8,128)(2,1)} %get-tuple-element.140) | copy-start | bytes 4718596 | tf_op jit(solution)/shard_map/while
  194.6 1.1 copy-start.8
  206.5 1.3 copy-start.13
  206.5 1.3 copy-start.16
  206.5 1.3 copy-start.17
  206.5 58.8 %copy-start.4 = (bf16[1,2,256,1536]{3,2,1,0:T(8,128)(2,1)S(1)}, bf16[1,2,256,1536]{3,2,1,0:T(8,128)(2,1)}, u32[]{:S(2)}) copy-start(bf16[1,2,256,1536]{3,2,1,0:T(8,128)(2,1)} %param.14) | copy-start | bytes 4718596
  206.6 99.5 %all-gather.13.cloned.1.call-start = ((), (), s32[]{:S(2)}) async-start(), calls=%async_computation.6 | async-start | bytes 10027008 | tf_op jit(solution)/shard_map/all_gather | solution.py:112
  207.2 180.5 %all-gather.15.cloned.1.call-start = ((), (), s32[]{:S(2)}) async-start(), calls=%async_computation.7 | async-start | bytes 10027008 | tf_op jit(solution)/shard_map/all_gather | solution.py:113
  207.7 225.0 %all-gather.11.cloned.1.call-start = ((), (), s32[]{:S(2)}) async-start(), calls=%async_computation.5 | async-start | bytes 4718592 | tf_op jit(solution)/shard_map/all_gather | solution.py:109
  267.4 238.9 %copy-start.2 = (bf16[2,256,1536]{2,1,0:T(8,128)(2,1)}, bf16[2,256,1536]{2,1,0:T(8,128)(2,1)S(1)}, u32[]{:S(2)}) copy-start(bf16[2,256,1536]{2,1,0:T(8,128)(2,1)S(1)} %get-tuple-element.65) | copy-start | bytes 4718596
  269.8 234.4 %reduce-scatter.5.cloned.1.call-start = ((), (), s32[]{:S(2)}) async-start(), calls=%async_computation.8 | async-start | bytes 4718592 | tf_op jit(solution)/shard_map/reduce_scatter | solution.py:115
  460.8 0.7 copy-start.12
  460.8 0.7 copy-start.14
  460.8 0.7 copy-start.15
  504.2 2.1 copy-start.5
  504.2 3.0 copy-start.19
  504.2 3.0 copy-start.20
  504.2 3.0 copy-start.21
  507.2 9.8 %copy-start.1 = (bf16[3,384,1536]{2,1,0:T(8,128)(2,1)S(1)}, bf16[3,384,1536]{2,1,0:T(8,128)(2,1)}, u32[]{:S(2)}) copy-start(bf16[3,384,1536]{2,1,0:T(8,128)(2,1)} %param.20) | copy-start | bytes 10616836
  509.9 0.7 copy-start.11
  511.2 4.2 collective-permute-start
Sparse Core Ops, SparseCore 0:
  44.5 17.4 all-gather.8
  63.6 46.3 all-gather.6
  206.7 58.6 reduce-scatter.2
Sparse Core Ops, SparseCore 1:
  209.3 96.7 all-gather.12
  308.2 79.4 all-gather.14
  389.1 43.6 all-gather.10
  460.9 43.2 reduce-scatter.4
where the time goes:
time: 527 us; the launch traced here: 524 us
  waiting for transfers between devices  318 us (60%)
  matrix products  115 us (22%)
  local copies, waits for them, and re-layouts  29.8 us (6%)
  other arithmetic  24.1 us (5%)
  blocking collectives  20.3 us (4%)
  between operations  15.7 us (3%)
    all_gather x1, waiting for transfers between devices, local(): lax.all_gather(w_down, ('req', 'seq'), axis=0, tiled=True)  81.6 us
    reduce_scatter x1, waiting for transfers between devices, local(): lax.psum_scatter(jnp.einsum('pnh,hd->npd', attended, w_attn_out, preferre...  57.5 us
    all_gather x1, waiting for transfers between devices, local(): both = lax.all_gather(own_rows, 'cfg', axis=0, tiled=True)  45.1 us
    reduce_scatter x1, waiting for transfers between devices, local(): lax.psum_scatter(partial_out.astype(jnp.bfloat16), 'cfg', scatter_dimensi...  42.1 us
    all_gather x1, waiting for transfers between devices, local(): lax.all_gather(a_img, 'seq', axis=1, tiled=True)  39.1 us
    sub x2, matrix products, attend(): probs = jax.nn.softmax(scores, axis=-1).astype(jnp.bfloat16)  36.8 us
    all_gather x1, waiting for transfers between devices, local(): lax.all_gather(w_up, ('req', 'seq'), axis=0, tiled=True)  36.2 us
    dot_general x1, matrix products, mlp_term(): return jnp.dot(hidden, down_block, preferred_element_type=jnp.float32)  28 us
  transfers between devices with their start and end apart: 8, of which 8 were waited for; matrix products, arithmetic and copies ran while one was open for 4% of the time, Pallas kernels for 0%

commit v1 on v0

--- a/solution.py
+++ b/solution.py
@@ -1,9 +1,14 @@
+import functools
+
 import jax
 import jax.numpy as jnp
 from jax import lax
+from jax.experimental import pallas as pl
+from jax.experimental.pallas import tpu as pltpu
 from jax.sharding import PartitionSpec as P
 
 HEAD = 64
+VMEM_BYTES = 56 * 1024 * 1024
 
 
 def partner_2(shard, axis, apart):
@@ -119,6 +124,301 @@
     resid_two = resid_one.astype(jnp.float32) + parts[:, 5] * mlp_out
     final_in = (layer_norm(resid_two) * (1.0 + parts[:, 9]) + parts[:, 8]).astype(jnp.bfloat16)
     branch_vel = jnp.einsum("pnd,dc->pnc", final_in, w_final, preferred_element_type=jnp.float32)
+    return guide(branch_vel, latent)
+
+def flip(shard, bits):
+    size = lax.axis_size("seq")
+    return lax.ppermute(shard, "seq", [(i, i ^ bits) for i in range(size)])
+
+
+def norm_rows(rows, scale, shift):
+    return (layer_norm(rows.astype(jnp.float32)) * (1.0 + scale) + shift).astype(jnp.bfloat16)
+
+
+def across(left, right):
+    return lax.dot_general(
+        left, right, (((1,), (1,)), ((), ())), preferred_element_type=jnp.float32
+    )
+
+
+def qkv_kernel(owners, img_rows, txt_rows, *refs):
+    count = len(owners)
+    pieces = refs[:count]
+    mod, w_img, w_txt, img_out, txt_out, txt_in = refs[count:]
+    for at, (piece, owner) in enumerate(zip(pieces, owners)):
+        img = norm_rows(piece[:img_rows], mod[owner, 1:2], mod[owner, 0:1])
+        img_out[pl.ds(at * img_rows, img_rows)] = across(img, w_img[...]).astype(jnp.bfloat16)
+        txt_in[pl.ds(at * txt_rows, txt_rows)] = norm_rows(
+            piece[img_rows:], mod[owner, 7:8], mod[owner, 6:7]
+        )
+    txt_out[...] = across(txt_in[...], w_txt[...]).astype(jnp.bfloat16)
+
+
+def project(pieces, owners, img_rows, parts, w_img, w_txt):
+    count = len(pieces)
+    txt_rows = pieces[0].shape[0] - img_rows
+    width = pieces[0].shape[1]
+    out = w_img.shape[0]
+    rows = count * (img_rows + txt_rows)
+    return pl.pallas_call(
+        functools.partial(qkv_kernel, owners, img_rows, txt_rows),
+        out_shape=(
+            jax.ShapeDtypeStruct((count * img_rows, out), jnp.bfloat16),
+            jax.ShapeDtypeStruct((count * txt_rows, out), jnp.bfloat16),
+        ),
+        in_specs=[pl.BlockSpec(memory_space=pltpu.VMEM)] * (count + 3),
+        out_specs=(pl.BlockSpec(memory_space=pltpu.VMEM),) * 2,
+        scratch_shapes=[pltpu.VMEM((count * txt_rows, width), jnp.bfloat16)],
+        compiler_params=pltpu.CompilerParams(vmem_limit_bytes=VMEM_BYTES),
+        cost_estimate=pl.CostEstimate(
+            flops=2 * rows * width * out, bytes_accessed=4 * out * width, transcendentals=0
+        ),
+    )(*pieces, parts, w_img, w_txt)
+
+
+def attend_kernel(
+    txt_rows, prompt, length, starts, qa, qb, ka, kb, va, vb, tka, tkb, tva, tvb, out
+):
+    first = lax.broadcasted_iota(jnp.int32, (1, 2 * HEAD), 1) < HEAD
+    column = lax.broadcasted_iota(jnp.int32, (1, 2 * txt_rows), 1)
+    live = []
+    for base in (0, 2):
+        slot = jnp.where(
+            column < txt_rows, starts[base] + column, starts[base + 1] + column - txt_rows
+        )
+        live.append(slot < length[prompt])
+    keys = (ka[...], kb[...], tka[...], tkb[...])
+    values = (va[...], vb[...], tva[...], tvb[...])
+    one = jnp.ones((), jnp.bfloat16)
+    zero = jnp.zeros((), jnp.bfloat16)
+    held = [
+        [jnp.where(first, value, one) for value in values],
+        [jnp.where(first, one, value) for value in values],
+    ]
+    for side, q_ref in enumerate((qa, qb)):
+        query = q_ref[...] * jnp.asarray(HEAD ** (-0.5), jnp.bfloat16)
+        sums = []
+        for head in range(2):
+            masked = jnp.where(first, query, zero) if head == 0 else jnp.where(first, zero, query)
+            scores = [across(masked, key) for key in keys]
+            for text in range(2):
+                scores[2 + text] = jnp.where(live[text], scores[2 + text], -1e30)
+            top = functools.reduce(
+                jnp.maximum, [jnp.max(score, axis=-1, keepdims=True) for score in scores]
+            )
+            total = None
+            for score, value in zip(scores, held[head]):
+                weight = jnp.exp(score - top).astype(jnp.bfloat16)
+                term = jnp.dot(weight, value, preferred_element_type=jnp.float32)
+                total = term if total is None else total + term
+            sums.append(total)
+        out[side] = jnp.where(
+            first, sums[0] / sums[0][:, HEAD : HEAD + 1], sums[1] / sums[1][:, 0:1]
+        ).astype(jnp.bfloat16)
+
+
+def attention(prompt, length, starts, near, far, img_rows):
+    img_near, txt_near = near
+    img_far, txt_far = far
+    lanes = 2 * HEAD
+    pairs = img_near.shape[1] // (3 * lanes)
+    txt_rows = txt_far.shape[0] // 2
+    half = 2 * img_rows
+    smem = pl.BlockSpec(memory_space=pltpu.SMEM)
+
+    def spec(rows, row_of, third):
+        return pl.BlockSpec((rows, lanes), lambda j, i: (row_of(i), third * pairs + j))
+
+    specs = [smem, smem]
+    specs += [spec(img_rows, lambda i: 2 * prompt + i, 0), spec(img_rows, lambda i: i, 0)]
+    for third in (1, 2):
+        specs += [spec(half, lambda i: prompt, third), spec(half, lambda i: 0, third)]
+    for third in (1, 2):
+        specs += [
+            spec(2 * txt_rows, lambda i: prompt, third),
+            spec(2 * txt_rows, lambda i: 0, third),
+        ]
+    keys = 2 * half + 4 * txt_rows
+    out = pl.pallas_call(
+        functools.partial(attend_kernel, txt_rows, prompt),
+        grid=(pairs, 2),
+        out_shape=jax.ShapeDtypeStruct((2, half, pairs * lanes), jnp.bfloat16),
+        in_specs=specs,
+        out_specs=pl.BlockSpec((2, img_rows, lanes), lambda j, i: (0, i, j)),
+        compiler_params=pltpu.CompilerParams(vmem_limit_bytes=VMEM_BYTES),
+        cost_estimate=pl.CostEstimate(
+            flops=16 * 2 * half * keys * pairs * lanes,
+            bytes_accessed=8 * half * pairs * lanes,
+            transcendentals=2 * half * keys * pairs * 2,
+        ),
+    )(
+        length, starts,
+        img_near, img_far, img_near, img_far, img_near, img_far,
+        txt_near, txt_far, txt_near, txt_far,
+    )
+    return out.reshape(2 * half, pairs * lanes)
+
+
+def tail_kernel(prompt, img_rows, *refs):
+    heads, outs, pieces = refs[0:4], refs[4:8], refs[8:12]
+    mod, up, down, keep, send, resid_out, state = refs[12:]
+    step = pl.program_id(0)
+    block = 2 * lax.rem(step, 2) + (1 - step // 2)
+    for at in range(4):
+
+        @pl.when(block == at)
+        def _():
+            state[...] = pieces[at][:img_rows]
+
+    proj = None
+    for head, weight in zip(heads, outs):
+        term = jnp.dot(head[...], weight[...], preferred_element_type=jnp.float32)
+        proj = term if proj is None else proj + term
+    resid = (state[...].astype(jnp.float32) + mod[prompt, 2:3] * proj).astype(jnp.bfloat16)
+
+    @pl.when(block == 0)
+    def _():
+        resid_out[...] = resid
+
+    normed = norm_rows(resid, mod[prompt, 4:5], mod[prompt, 3:4])
+    hidden_units = up.shape[0]
+    cut = 512
+    total = None
+    for start in range(0, hidden_units, cut):
+        inner = across(normed, up[pl.ds(start, cut)])
+        hidden = jax.nn.gelu(inner, approximate=True).astype(jnp.bfloat16)
+        term = jnp.dot(hidden, down[pl.ds(start, cut)], preferred_element_type=jnp.float32)
+        total = term if total is None else total + term
+    total = total.astype(jnp.bfloat16)
+
+    @pl.when(step < 2)
+    def _():
+        send[...] = total
+
+    @pl.when(step >= 2)
+    def _():
+        keep[...] = total
+
+
+def tail(prompt, heads, outs, pieces, parts, up, down, img_rows):
+    width = up.shape[1]
+    local_width = heads[0].shape[1]
+
+    def block_of(step):
+        return 2 * lax.rem(step, 2) + (1 - step // 2)
+
+    def spec(flipped):
+        return pl.BlockSpec((img_rows, local_width), lambda t: (block_of(t) ^ flipped, 0))
+
+    vmem = pl.BlockSpec(memory_space=pltpu.VMEM)
+    rows = 4 * img_rows
+    return pl.pallas_call(
+        functools.partial(tail_kernel, prompt, img_rows),
+        grid=(4,),
+        out_shape=(
+            jax.ShapeDtypeStruct((2 * img_rows, width), jnp.bfloat16),
+            jax.ShapeDtypeStruct((2 * img_rows, width), jnp.bfloat16),
+            jax.ShapeDtypeStruct((img_rows, width), jnp.bfloat16),
+        ),
+        in_specs=[spec(r) for r in range(4)] + [vmem] * 11,
+        out_specs=(
+            pl.BlockSpec((img_rows, width), lambda t: (jnp.maximum(t - 2, 0), 0)),
+            pl.BlockSpec((img_rows, width), lambda t: (jnp.minimum(t, 1), 0)),
+            pl.BlockSpec((img_rows, width), lambda t: (0, 0)),
+        ),
+        scratch_shapes=[pltpu.VMEM((img_rows, width), jnp.bfloat16)],
+        compiler_params=pltpu.CompilerParams(vmem_limit_bytes=VMEM_BYTES),
+        cost_estimate=pl.CostEstimate(
+            flops=2 * rows * width * (width + 2 * up.shape[0]),
+            bytes_accessed=2 * width * (width + 2 * up.shape[0]) + 8 * rows * width,
+            transcendentals=rows * up.shape[0],
+        ),
+    )(*heads, *outs, *pieces, parts, up, down)
+
+
+def final_kernel(prompts, img_rows, *refs):
+    mod, w_final, out = refs[4 * prompts :]
+    for prompt in range(prompts):
+        resid, keep, core, chip = refs[4 * prompt : 4 * prompt + 4]
+        mlp = (
+            keep[:img_rows].astype(jnp.float32)
+            + core[:img_rows].astype(jnp.float32)
+            + chip[...].astype(jnp.float32)
+        )
+        two = resid[...].astype(jnp.float32) + mod[prompt, 5:6] * mlp
+        last = (layer_norm(two) * (1.0 + mod[prompt, 9:10]) + mod[prompt, 8:9]).astype(
+            jnp.bfloat16
+        )
+        out[prompt] = jnp.dot(last, w_final[...], preferred_element_type=jnp.float32)
+
+
+def fast(
+    img_state,
+    txt_state,
+    cond_vec,
+    text_len,
+    latent,
+    w_mod,
+    w_qkv_img,
+    w_qkv_txt,
+    w_attn_out,
+    w_up,
+    w_down,
+    w_final,
+):
+    prompts = img_state.shape[1]
+    img_rows = img_state.shape[2]
+    txt_rows = txt_state.shape[2]
+    width = img_state.shape[3]
+    own = [jnp.concatenate([img_state[0, p], txt_state[0, p]], axis=0) for p in range(prompts)]
+    pieces = [[rows, flip(rows, 1), flip(rows, 2)] for rows in own]
+    for rows in pieces:
+        rows.append(flip(rows[2], 1))
+    up = lax.all_gather(w_up, ("cfg", "req"), axis=0, tiled=True)
+    down = lax.all_gather(w_down, ("cfg", "req"), axis=0, tiled=True)
+    cond_act = jax.nn.silu(cond_vec[0]).astype(jnp.bfloat16)
+    mod_part = across(cond_act, w_mod)
+    mod_all = lax.all_gather(mod_part, ("req", "seq"), axis=1, tiled=True)
+    mine = lax.dynamic_slice_in_dim(mod_all, lax.axis_index("req") * prompts, prompts, 0)
+    parts = mine.reshape(prompts, 10, width)
+    w_img = w_qkv_img.reshape(-1, width)
+    w_txt = w_qkv_txt.reshape(-1, width)
+    me = lax.axis_index("seq")
+    starts = jnp.stack([txt_rows * (me ^ r) for r in range(4)]).astype(jnp.int32)
+    near = project(
+        [rows[r] for rows in pieces for r in (0, 1)],
+        [p for p in range(prompts) for r in (0, 1)],
+        img_rows, parts, w_img, w_txt,
+    )
+    outs = [w_attn_out, flip(w_attn_out, 1), flip(w_attn_out, 2)]
+    outs.append(flip(outs[2], 1))
+    results = []
+    for p in range(prompts):
+        far = project(pieces[p][2:], [p, p], img_rows, parts, w_img, w_txt)
+        own_heads = attention(p, text_len[0], starts, near, far, img_rows)
+        heads = [own_heads, flip(own_heads, 1), flip(own_heads, 2)]
+        heads.append(flip(heads[2], 1))
+        keep, send, resid = tail(p, heads, outs, pieces[p], parts, up, down, img_rows)
+        core = flip(send, 1)
+        chip = flip(
+            (keep[img_rows:].astype(jnp.float32) + core[img_rows:].astype(jnp.float32)).astype(
+                jnp.bfloat16
+            ),
+            2,
+        )
+        results += [resid, keep, core, chip]
+    vmem = pl.BlockSpec(memory_space=pltpu.VMEM)
+    branch_vel = pl.pallas_call(
+        functools.partial(final_kernel, prompts, img_rows),
+        out_shape=jax.ShapeDtypeStruct((prompts, img_rows, w_final.shape[1]), jnp.float32),
+        in_specs=[vmem] * (4 * prompts + 2),
+        out_specs=vmem,
+        compiler_params=pltpu.CompilerParams(vmem_limit_bytes=VMEM_BYTES),
+    )(*results, parts, w_final)
+    return guide(branch_vel, latent)
+
+
+def guide(branch_vel, latent):
     half_width = latent.shape[2]
     branch_index = lax.axis_index("cfg")
     own_half = lax.dynamic_slice_in_dim(branch_vel, branch_index * half_width, half_width, 2)
@@ -132,6 +432,17 @@
     velocity = uncond_vel + 4.5 * (cond_vel - uncond_vel)
     latent_next = latent - 0.04 * velocity
     return (velocity, latent_next)
+
+
+def plan(*shards):
+    img_state, txt_state, w_qkv_img = shards[0], shards[1], shards[6]
+    fits = (
+        lax.axis_size("seq") == 4
+        and img_state.shape[2] % 128 == 0
+        and txt_state.shape[2] % 16 == 0
+        and w_qkv_img.shape[1] % (2 * HEAD) == 0
+    )
+    return fast(*shards) if fits else local(*shards)
 
 
 def solution(mesh):
@@ -150,7 +461,7 @@
         P(),
     )
     return jax.shard_map(
-        local,
+        plan,
         mesh=mesh,
         in_specs=placed,
         out_specs=(P("req", "seq", "cfg"), P("req", "seq", "cfg")),

time: 527 us -> 312 us (0.59)
  waiting for transfers between devices: 318 us -> 53.5 us
  Pallas kernels: 0 us -> 130 us
  matrix products: 115 us -> 0.85 us
  blocking collectives: 20.3 us -> 77.3 us
  local copies, waits for them, and re-layouts: 29.8 us -> 12.2 us
  other arithmetic: 24.1 us -> 6.74 us
  starting transfers between devices: 0.85 us -> 13.7 us
    all_gather x5 -> x2, waiting for transfers between devices: 214 us -> 0.01 us  [the longest x1 0.01 us: fast(): up = lax.all_gather(w_up, ('cfg', 'req'), axis=0, tiled=True)]
    pallas_call x0 -> x8, Pallas kernels: none -> 130 us  [the longest x2 59.2 us: tail(): pl.pallas_call(functools.partial(tail_kernel, prompt, img_rows), grid=(4,...]
    reduce_scatter x2 -> x0, waiting for transfers between devices: 99.6 us -> none  [the longest x1 57.5 us: local(): lax.psum_scatter(jnp.einsum('pnh,hd->npd', attended, w_attn_out, preferre...]
    dot_general x8 -> x1, matrix products: 78.5 us -> 0.85 us  [across(): lax.dot_general(left, right, (((1,), (1,)), ((), ())), preferred_element_...]
    all_gather x1, blocking collectives: 20.3 us -> 77.3 us  [fast(): mod_all = lax.all_gather(mod_part, ('req', 'seq'), axis=1, tiled=True)]
    ppermute x0 -> x19, waiting for transfers between devices: none -> 48.7 us  [flip(): return lax.ppermute(shard, 'seq', [(i, i ^ bits) for i in range(size)])]
    sub x2 -> x0, matrix products: 36.8 us -> none  [attend(): probs = jax.nn.softmax(scores, axis=-1).astype(jnp.bfloat16)]
    ppermute x0 -> x19, starting transfers between devices: none -> 12.1 us  [flip(): return lax.ppermute(shard, 'seq', [(i, i ^ bits) for i in range(size)])]
  transfers between devices with their start and end apart: 8 -> 22, of which waited for: 8 -> 5; matrix products, arithmetic and copies ran while one was open for 4% -> 4% of each run, Pallas kernels for 0% -> 40%
where the time goes in v1:
time: 312 us; the launch traced here: 308 us
  Pallas kernels  130 us (42%)
  blocking collectives  77.3 us (25%)
  waiting for transfers between devices  53.5 us (17%)
  between operations  14.2 us (5%)
  starting transfers between devices  13.7 us (4%)
  local copies, waits for them, and re-layouts  12.2 us (4%)
  other arithmetic  6.74 us (2%)
    all_gather x1, blocking collectives, fast(): mod_all = lax.all_gather(mod_part, ('req', 'seq'), axis=1, tiled=True)  77.3 us
    pallas_call x2, Pallas kernels, tail(): pl.pallas_call(functools.partial(tail_kernel, prompt, img_rows), grid=(4,...  59.2 us
    ppermute x19, waiting for transfers between devices, flip(): return lax.ppermute(shard, 'seq', [(i, i ^ bits) for i in range(size)])  48.7 us
    pallas_call x2, Pallas kernels, attention(): pl.pallas_call(functools.partial(attend_kernel, txt_rows, prompt), grid=(...  35.9 us
    pallas_call x3, Pallas kernels, project(): pl.pallas_call(functools.partial(qkv_kernel, owners, img_rows, txt_rows),...  28 us
    ppermute x19, starting transfers between devices, flip(): return lax.ppermute(shard, 'seq', [(i, i ^ bits) for i in range(size)])  12.1 us
    pallas_call x1, Pallas kernels, fast(): pl.pallas_call(functools.partial(final_kernel, prompts, img_rows), out_sh...  6.53 us
    unnamed x29, local copies, waits for them, and re-layouts  6.5 us
  transfers between devices with their start and end apart: 22, of which 5 were waited for; matrix products, arithmetic and copies ran while one was open for 4% of the time, Pallas kernels for 40%

profile of v1, /device:TPU:8, one launch (start us, length us, event | category | flops | bytes accessed | tf_op | source)
XLA Modules:
  0.0 308.1 jit_solution(10255307623703269220)
XLA Ops:
  7.2 0.0 copy-start
  7.2 0.0 all-gather.4.cloned.1.call-start
  7.2 0.7 all-gather.4.cloned.1.call-update
  7.9 0.0 all-gather.6.cloned.1.call-start
  8.0 0.7 all-gather.6.cloned.1.call-update
  8.7 1.0 slice_bitcast_fusion.2
  9.7 1.5 slice_bitcast_fusion
  11.1 0.0 copy-start.8
  11.2 1.0 pad_maximum_fusion.1.refs_2_.refs_8_
  12.2 1.5 collective-permute-start.12
  13.7 0.0 collective-permute-start.1
  13.7 1.0 pad_maximum_fusion.refs_0_.refs_8_
  14.7 0.5 collective-permute-start
  15.2 0.5 collective-permute-start.2
  15.7 1.5 collective-permute-start.8
  17.2 0.9 convolution_bitcast_fusion
  18.1 77.3 %all-gather = f32[16,960,8]{1,2,0:T(8,128)S(1)} all-gather(f32[1,960,8]{1,2,0:T(8,128)S(1)} %convolution_bitcast_fusion), channel_id=1, replica_groups=mesh['cfg'=2,'req'=4,'seq'=4] {'req','seq'}, dimensions={0}, use_global_device_ids=true | all-gather | bytes 522240 | tf_op jit(solution)/shard_map/all_gather | solution.py:381
  95.4 0.3 copy.23
  95.7 1.0 reshape.25
  96.7 0.0 collective-permute-done.12.refs_0_.refs_10_
  96.7 0.3 collective-permute-start.13
  97.1 1.1 dynamic-slice_bitcast_fusion
  98.1 0.8 reshape.19.refs_4_.refs_2_.refs_12_.refs_8_
  98.9 0.6 pad_add_fusion.starts
  99.5 0.0 collective-permute-done.refs_1_.refs_9_
  99.5 0.2 collective-permute-start.7
  99.7 0.0 collective-permute-done.2.refs_0_.refs_10_
  99.7 0.3 collective-permute-start.3
  100.0 0.0 collective-permute-done.1.refs_3_.refs_9_
  100.0 11.7 %shard_map.131 = (bf16[1024,1152]{1,0:T(8,128)(2,1)}, bf16[192,1152]{1,0:T(8,128)(2,1)}) custom-call(bf16[304,1536]{1,0:T(8,128)(2,1)} %pad_maximum_fusion.refs_0_.refs_8_, bf16[304,1536]{1,0:T(8,128)(2,1)} %collective-permute-done.refs_1_.refs_9_, bf16[304,1536]{1,0:T(8,128)(2,1)} %pad_maximum_fusion.1.refs_2_.refs_8_, ...), custom_call_target="tpu_custom_call" | custom-call | flops 4303355904 | bytes 7077888 | tf_op jit(solution)/shard_map/pallas_call | solution.py:163
  111.7 0.0 collective-permute-done.8.refs_6_
  111.7 0.2 collective-permute-start.9
  111.9 8.2 %shard_map.135 = (bf16[512,1152]{1,0:T(8,128)(2,1)}, bf16[96,1152]{1,0:T(8,128)(2,1)}) custom-call(bf16[304,1536]{1,0:T(8,128)(2,1)} %collective-permute-done.12.refs_0_.refs_10_, bf16[304,1536]{1,0:T(8,128)(2,1)} %collective-permute-done.13.refs_1_.refs_11_, f32[2,10,1536]{2,1,0:T(8,128)} %reshape.19.refs_4_.refs_2_.refs_12_.refs_8_, ...), custom_call_target="tpu_custom_call" | custom-call | flops 2151677952 | bytes 7077888 | tf_op jit(solution)/shard_map/pallas_call | solution.py:163
  120.1 18.0 %shard_map.136 = bf16[2,512,384]{2,1,0:T(8,128)(2,1)} custom-call(s32[2]{0:T(128)} %bitcast.52, s32[4]{0:T(128)} %pad_add_fusion.starts, bf16[1024,1152]{1,0:T(8,128)(2,1)} %get-tuple-element.14.qa.ka.va, bf16[512,1152]{1,0:T(8,128)(2,1)} %get-tuple-element.21.qb.kb.vb, bf16[1024,1152]{1,0:T(8,128)(2,1)} %get-tuple-element.14.qa.ka.va, ...), custom_call_target="tpu_custom_call" | custom-call | flops 7650410496 | bytes 1572864 | tf_op jit(solution)/shard_map/pallas_call | solution.py:242
  138.1 0.1 collective-permute-start.15
  138.2 0.9 copy-done.5
  139.1 8.1 %shard_map.132 = (bf16[512,1152]{1,0:T(8,128)(2,1)}, bf16[96,1152]{1,0:T(8,128)(2,1)}) custom-call(bf16[304,1536]{1,0:T(8,128)(2,1)} %collective-permute-done.2.refs_0_.refs_10_, bf16[304,1536]{1,0:T(8,128)(2,1)} %copy-done.5, f32[2,10,1536]{2,1,0:T(8,128)} %reshape.19.refs_4_.refs_2_.refs_12_.refs_8_, bf16[1152,1536]{1,0:T(8,128)(2,1)} %bitcast.42, ...), custom_call_target="tpu_custom_call" | custom-call | flops 2151677952 | bytes 7077888 | tf_op jit(solution)/shard_map/pallas_call | solution.py:163
  147.3 17.9 %shard_map.133 = bf16[2,512,384]{2,1,0:T(8,128)(2,1)} custom-call(s32[2]{0:T(128)} %bitcast.53, s32[4]{0:T(128)} %pad_add_fusion.starts, bf16[1024,1152]{1,0:T(8,128)(2,1)} %get-tuple-element.14.qa.ka.va, bf16[512,1152]{1,0:T(8,128)(2,1)} %get-tuple-element.15.qb.kb.vb, bf16[1024,1152]{1,0:T(8,128)(2,1)} %get-tuple-element.14.qa.ka.va, ...), custom_call_target="tpu_custom_call" | custom-call | flops 7650410496 | bytes 1572864 | tf_op jit(solution)/shard_map/pallas_call | solution.py:242
  165.1 2.1 collective-permute-start.5
  167.2 0.5 collective-permute-start.16
  167.7 0.1 collective-permute-start.4
  167.8 17.5 %collective-permute-done.5.refs_2_ = bf16[1024,384]{1,0:T(8,128)(2,1)} collective-permute-done((bf16[1024,384]{1,0:T(8,128)(2,1)}, bf16[1024,384]{1,0:T(8,128)(2,1)}, u32[]{:S(2)}, u32[]{:S(2)}) %collective-permute-start.5) | collective-permute-done | bytes 786464 | tf_op jit(solution)/shard_map/ppermute | solution.py:131
  185.3 0.9 copy-done.11
  186.2 29.7 %shard_map.137 = (bf16[512,1536]{1,0:T(8,128)(2,1)}, bf16[512,1536]{1,0:T(8,128)(2,1)}, bf16[256,1536]{1,0:T(8,128)(2,1)}) custom-call(bf16[1024,384]{1,0:T(8,128)(2,1)} %bitcast.50, bf16[1024,384]{1,0:T(8,128)(2,1)} %copy-done.11, bf16[1024,384]{1,0:T(8,128)(2,1)} %copy-done.10, bf16[1024,384]{1,0:T(8,128)(2,1)} %collective-permute-done.16.refs_3_, ...), custom_call_target="tpu_custom_call" | custom-call | flops 14495514624 | bytes 26738688 | tf_op jit(solution)/shard_map/pallas_call | solution.py:315
  215.9 0.6 collective-permute-start.17
  216.5 29.5 %shard_map.134 = (bf16[512,1536]{1,0:T(8,128)(2,1)}, bf16[512,1536]{1,0:T(8,128)(2,1)}, bf16[256,1536]{1,0:T(8,128)(2,1)}) custom-call(bf16[1024,384]{1,0:T(8,128)(2,1)} %bitcast.48, bf16[1024,384]{1,0:T(8,128)(2,1)} %collective-permute-done.4.refs_1_, bf16[1024,384]{1,0:T(8,128)(2,1)} %collective-permute-done.5.refs_2_, ...), custom_call_target="tpu_custom_call" | custom-call | flops 14495514624 | bytes 26738688 | tf_op jit(solution)/shard_map/pallas_call | solution.py:315
  246.0 0.2 collective-permute-start.10
  246.2 1.1 add_convert_fusion
  247.3 1.8 collective-permute-start.18
  249.0 0.6 collective-permute-done.10.refs_2_
  249.7 1.2 add_convert_fusion.1
  250.9 0.2 copy-done.4
  251.1 1.7 collective-permute-start.11
  252.8 0.9 copy.24.refs_9_
  253.7 14.2 %collective-permute-done.18.refs_7_ = bf16[256,1536]{1,0:T(8,128)(2,1)} collective-permute-done((bf16[256,1536]{1,0:T(8,128)(2,1)}, bf16[256,1536]{1,0:T(8,128)(2,1)}, u32[]{:S(2)}, u32[]{:S(2)}) %collective-permute-start.18) | collective-permute-done | bytes 786464 | tf_op jit(solution)/shard_map/ppermute | solution.py:131
  268.0 16.3 %collective-permute-done.11.refs_3_ = bf16[256,1536]{1,0:T(8,128)(2,1)} collective-permute-done((bf16[256,1536]{1,0:T(8,128)(2,1)}, bf16[256,1536]{1,0:T(8,128)(2,1)}, u32[]{:S(2)}, u32[]{:S(2)}) %collective-permute-start.11) | collective-permute-done | bytes 786464 | tf_op jit(solution)/shard_map/ppermute | solution.py:131
  284.3 6.5 %shard_map.138 = f32[2,256,64]{2,1,0:T(8,128)} custom-call(bf16[256,1536]{1,0:T(8,128)(2,1)} %get-tuple-element.18.refs_0_, bf16[512,1536]{1,0:T(8,128)(2,1)} %get-tuple-element.19.refs_1_, bf16[512,1536]{1,0:T(8,128)(2,1)} %copy-done.4, bf16[256,1536]{1,0:T(8,128)(2,1)} %collective-permute-done.11.refs_3_, bf16[256,1536]{1,0:T(8,128)(2,1)} %get-tuple-element.23.refs_4_, ...), custom_call_target="tpu_custom_call" | custom-call | tf_op jit(solution)/shard_map/pallas_call | solution.py:411
  290.8 1.0 dynamic-slice_convert_fusion
  291.9 1.6 collective-permute-start.19
  293.4 0.1 copy.25
  293.6 3.5 %collective-permute-done.19 = bf16[2,256,32]{2,1,0:T(8,128)(2,1)} collective-permute-done((bf16[2,256,32]{2,1,0:T(8,128)(2,1)S(1)}, bf16[2,256,32]{2,1,0:T(8,128)(2,1)}, u32[]{:S(2)}, u32[]{:S(2)}) %collective-permute-start.19) | collective-permute-done | bytes 32800 | tf_op jit(solution)/shard_map/ppermute | solution.py:15
  297.0 1.8 multiply_subtract_fusion
  298.8 1.7 copy.26
  300.5 0.7 copy.27
  (33 shorter events, 0.1 us)
Async XLA Ops:
  7.2 10.1 %copy-start = (bf16[960,1536]{1,0:T(8,128)(2,1)S(1)}, bf16[960,1536]{1,0:T(8,128)(2,1)}, u32[]{:S(2)}) copy-start(bf16[960,1536]{1,0:T(8,128)(2,1)} %param.17) | copy-start | bytes 8847364
  7.2 179.0 %all-gather.4.cloned.1.call-start = ((), (), s32[]{:S(2)}) async-start(), calls=%async_computation | async-start | bytes 5308416 | tf_op jit(solution)/shard_map/all_gather | solution.py:377
  7.9 178.3 %all-gather.6.cloned.1.call-start = ((), (), s32[]{:S(2)}) async-start(), calls=%async_computation.1 | async-start | bytes 5308416 | tf_op jit(solution)/shard_map/all_gather | solution.py:378
  11.1 6.1 %copy-start.8 = (f32[1,8,1536]{2,1,0:T(8,128)S(1)}, f32[1,8,1536]{2,1,0:T(8,128)}, u32[]{:S(2)}) copy-start(f32[1,8,1536]{2,1,0:T(8,128)} %param.14) | copy-start | bytes 147460
  12.2 84.5 %collective-permute-start.12 = (bf16[304,1536]{1,0:T(8,128)(2,1)}, bf16[304,1536]{1,0:T(8,128)(2,1)}, u32[]{:S(2)}, u32[]{:S(2)}) collective-permute-start(bf16[304,1536]{1,0:T(8,128)(2,1)} %pad_maximum_fusion.1.refs_2_.refs_8_), channel_id=1, source_target_pairs={{0,2},{1,3},{2,0},{3,1},{4,6},{5,7},{6,4},{7,5},{8,10},{9,11},{10,... | collective-permute-start | bytes 2801672 | tf_op jit(solution)/shard_map/ppermute | solution.py:131
  13.7 86.3 %collective-permute-start.1 = (bf16[304,1536]{1,0:T(8,128)(2,1)}, bf16[304,1536]{1,0:T(8,128)(2,1)}, u32[]{:S(2)}, u32[]{:S(2)}) collective-permute-start(bf16[304,1536]{1,0:T(8,128)(2,1)} %pad_maximum_fusion.1.refs_2_.refs_8_), channel_id=1, source_target_pairs={{0,1},{1,0},{2,3},{3,2},{4,5},{5,4},{6,7},{7,6},{8,9},{9,8},{10,11... | collective-permute-start | bytes 2801672 | tf_op jit(solution)/shard_map/ppermute | solution.py:131
  14.7 84.8 %collective-permute-start = (bf16[304,1536]{1,0:T(8,128)(2,1)}, bf16[304,1536]{1,0:T(8,128)(2,1)}, u32[]{:S(2)}, u32[]{:S(2)}) collective-permute-start(bf16[304,1536]{1,0:T(8,128)(2,1)} %pad_maximum_fusion.refs_0_.refs_8_), channel_id=1, source_target_pairs={{0,1},{1,0},{2,3},{3,2},{4,5},{5,4},{6,7},{7,6},{8,9},{9,8},{10,11... | collective-permute-start | bytes 2801672 | tf_op jit(solution)/shard_map/ppermute | solution.py:131
  15.2 84.4 %collective-permute-start.2 = (bf16[304,1536]{1,0:T(8,128)(2,1)}, bf16[304,1536]{1,0:T(8,128)(2,1)}, u32[]{:S(2)}, u32[]{:S(2)}) collective-permute-start(bf16[304,1536]{1,0:T(8,128)(2,1)} %pad_maximum_fusion.refs_0_.refs_8_), channel_id=1, source_target_pairs={{0,2},{1,3},{2,0},{3,1},{4,6},{5,7},{6,4},{7,5},{8,10},{9,11},{10,... | collective-permute-start | bytes 2801672 | tf_op jit(solution)/shard_map/ppermute | solution.py:131
  15.7 96.0 %collective-permute-start.8 = (bf16[384,1536]{1,0:T(8,128)(2,1)}, bf16[384,1536]{1,0:T(8,128)(2,1)}, u32[]{:S(2)}, u32[]{:S(2)}) collective-permute-start(bf16[384,1536]{1,0:T(8,128)(2,1)} %refs_4_.3), channel_id=1, source_target_pairs={{0,2},{1,3},{2,0},{3,1},{4,6},{5,7},{6,4},{7,5},{8,10},{9,11},{10,... | collective-permute-start | bytes 3538952 | tf_op jit(solution)/shard_map/ppermute | solution.py:131
  96.7 15.1 %collective-permute-start.13 = (bf16[304,1536]{1,0:T(8,128)(2,1)}, bf16[304,1536]{1,0:T(8,128)(2,1)}, u32[]{:S(2)}, u32[]{:S(2)}) collective-permute-start(bf16[304,1536]{1,0:T(8,128)(2,1)} %collective-permute-done.12.refs_0_.refs_10_), channel_id=1, source_target_pairs={{0,1},{1,0},{2,3},{3,2},{4,5},{5,4},{6,7},{7,6},{8,9},{9,8},{10,11... | collective-permute-start | bytes 2801672 | tf_op jit(solution)/shard_map/ppermute | solution.py:131
  99.5 68.2 %collective-permute-start.7 = (bf16[384,1536]{1,0:T(8,128)(2,1)}, bf16[384,1536]{1,0:T(8,128)(2,1)}, u32[]{:S(2)}, u32[]{:S(2)}) collective-permute-start(bf16[384,1536]{1,0:T(8,128)(2,1)} %refs_4_.3), channel_id=1, source_target_pairs={{0,1},{1,0},{2,3},{3,2},{4,5},{5,4},{6,7},{7,6},{8,9},{9,8},{10,11... | collective-permute-start | bytes 3538952 | tf_op jit(solution)/shard_map/ppermute | solution.py:131
  99.7 38.5 %collective-permute-start.3 = (bf16[304,1536]{1,0:T(8,128)(2,1)}, bf16[304,1536]{1,0:T(8,128)(2,1)S(1)}, u32[]{:S(2)}, u32[]{:S(2)}) collective-permute-start(bf16[304,1536]{1,0:T(8,128)(2,1)} %collective-permute-done.2.refs_0_.refs_10_), channel_id=1, source_target_pairs={{0,1},{1,0},{2,3},{3,2},{4,5},{5,4},{6,7},{7,6},{8,9},{9,8},{10,11... | collective-permute-start | bytes 2801672 | tf_op jit(solution)/shard_map/ppermute | solution.py:131
  111.7 73.6 %collective-permute-start.9 = (bf16[384,1536]{1,0:T(8,128)(2,1)}, bf16[384,1536]{1,0:T(8,128)(2,1)}, u32[]{:S(2)}, u32[]{:S(2)}) collective-permute-start(bf16[384,1536]{1,0:T(8,128)(2,1)} %collective-permute-done.8.refs_6_), channel_id=1, source_target_pairs={{0,1},{1,0},{2,3},{3,2},{4,5},{5,4},{6,7},{7,6},{8,9},{9,8},{10,11... | collective-permute-start | bytes 3538952 | tf_op jit(solution)/shard_map/ppermute | solution.py:131
  138.1 29.1 %collective-permute-start.15 = (bf16[1024,384]{1,0:T(8,128)(2,1)}, bf16[1024,384]{1,0:T(8,128)(2,1)S(1)}, u32[]{:S(2)}, u32[]{:S(2)}) collective-permute-start(bf16[1024,384]{1,0:T(8,128)(2,1)} %bitcast.49), channel_id=1, source_target_pairs={{0,2},{1,3},{2,0},{3,1},{4,6},{5,7},{6,4},{7,5},{8,10},{9,11},{10,... | collective-permute-start | bytes 2359304 | tf_op jit(solution)/shard_map/ppermute | solution.py:131
  138.2 0.9 copy-start.5
  147.3 19.9 %copy-start.9 = (bf16[2,512,384]{2,1,0:T(8,128)(2,1)S(1)}, bf16[2,512,384]{2,1,0:T(8,128)(2,1)}, u32[]{:S(2)}) copy-start(bf16[2,512,384]{2,1,0:T(8,128)(2,1)} %shard_map.136) | copy-start | bytes 2359300
  165.1 20.2 %collective-permute-start.5 = (bf16[1024,384]{1,0:T(8,128)(2,1)}, bf16[1024,384]{1,0:T(8,128)(2,1)}, u32[]{:S(2)}, u32[]{:S(2)}) collective-permute-start(bf16[1024,384]{1,0:T(8,128)(2,1)} %bitcast.46), channel_id=1, source_target_pairs={{0,2},{1,3},{2,0},{3,1},{4,6},{5,7},{6,4},{7,5},{8,10},{9,11},{10,... | collective-permute-start | bytes 2359304 | tf_op jit(solution)/shard_map/ppermute | solution.py:131
  167.2 18.1 %collective-permute-start.14 = (bf16[1024,384]{1,0:T(8,128)(2,1)S(1)}, bf16[1024,384]{1,0:T(8,128)(2,1)S(1)}, u32[]{:S(2)}, u32[]{:S(2)}) collective-permute-start(bf16[1024,384]{1,0:T(8,128)(2,1)S(1)} %bitcast.51), channel_id=1, source_target_pairs={{0,1},{1,0},{2,3},{3,2},{4,5},{5,4},{6,7},{7,6},{8,9},{9,8},{10,11... | collective-permute-start | bytes 2359304 | tf_op jit(solution)/shard_map/ppermute | solution.py:131
  167.2 18.1 %copy-start.10 = (bf16[1024,384]{1,0:T(8,128)(2,1)}, bf16[1024,384]{1,0:T(8,128)(2,1)S(1)}, u32[]{:S(2)}) copy-start(bf16[1024,384]{1,0:T(8,128)(2,1)S(1)} %collective-permute-done.15.refs_2_) | copy-start | bytes 2359300
  167.2 19.0 %collective-permute-start.16 = (bf16[1024,384]{1,0:T(8,128)(2,1)S(1)}, bf16[1024,384]{1,0:T(8,128)(2,1)}, u32[]{:S(2)}, u32[]{:S(2)}) collective-permute-start(bf16[1024,384]{1,0:T(8,128)(2,1)S(1)} %collective-permute-done.15.refs_2_), channel_id=1, source_target_pairs={{0,1},{1,0},{2,3},{3,2},{4,5},{5,4},{6,7},{7,6},{8,9},{9,8},{10,11... | collective-permute-start | bytes 2359304 | tf_op jit(solution)/shard_map/ppermute | solution.py:131
  167.7 48.7 %collective-permute-start.4 = (bf16[1024,384]{1,0:T(8,128)(2,1)}, bf16[1024,384]{1,0:T(8,128)(2,1)}, u32[]{:S(2)}, u32[]{:S(2)}) collective-permute-start(bf16[1024,384]{1,0:T(8,128)(2,1)} %bitcast.47), channel_id=1, source_target_pairs={{0,1},{1,0},{2,3},{3,2},{4,5},{5,4},{6,7},{7,6},{8,9},{9,8},{10,11... | collective-permute-start | bytes 2359304 | tf_op jit(solution)/shard_map/ppermute | solution.py:131
  185.3 31.2 %collective-permute-start.6 = (bf16[1024,384]{1,0:T(8,128)(2,1)}, bf16[1024,384]{1,0:T(8,128)(2,1)}, u32[]{:S(2)}, u32[]{:S(2)}) collective-permute-start(bf16[1024,384]{1,0:T(8,128)(2,1)} %collective-permute-done.5.refs_2_), channel_id=1, source_target_pairs={{0,1},{1,0},{2,3},{3,2},{4,5},{5,4},{6,7},{7,6},{8,9},{9,8},{10,11... | collective-permute-start | bytes 2359304 | tf_op jit(solution)/shard_map/ppermute | solution.py:131
  185.3 0.9 copy-start.11
  215.9 30.3 %copy-start.1 = (bf16[512,1536]{1,0:T(8,128)(2,1)S(1)}, bf16[512,1536]{1,0:T(8,128)(2,1)}, u32[]{:S(2)}) copy-start(bf16[512,1536]{1,0:T(8,128)(2,1)} %get-tuple-element.24.refs_5_) | copy-start | bytes 4718596
  215.9 30.3 %collective-permute-start.17 = (bf16[512,1536]{1,0:T(8,128)(2,1)}, bf16[512,1536]{1,0:T(8,128)(2,1)S(1)}, u32[]{:S(2)}, u32[]{:S(2)}) collective-permute-start(bf16[512,1536]{1,0:T(8,128)(2,1)} %get-tuple-element.25), channel_id=1, source_target_pairs={{0,1},{1,0},{2,3},{3,2},{4,5},{5,4},{6,7},{7,6},{8,9},{9,8},{10,11... | collective-permute-start | bytes 4718600 | tf_op jit(solution)/shard_map/ppermute | solution.py:131
  246.0 3.7 %copy-start.3 = (bf16[512,1536]{1,0:T(8,128)(2,1)S(1)}, bf16[512,1536]{1,0:T(8,128)(2,1)}, u32[]{:S(2)}) copy-start(bf16[512,1536]{1,0:T(8,128)(2,1)} %get-tuple-element.19.refs_1_) | copy-start | bytes 4718596
  246.0 3.7 %collective-permute-start.10 = (bf16[512,1536]{1,0:T(8,128)(2,1)}, bf16[512,1536]{1,0:T(8,128)(2,1)S(1)}, u32[]{:S(2)}, u32[]{:S(2)}) collective-permute-start(bf16[512,1536]{1,0:T(8,128)(2,1)} %get-tuple-element.20), channel_id=1, source_target_pairs={{0,1},{1,0},{2,3},{3,2},{4,5},{5,4},{6,7},{7,6},{8,9},{9,8},{10,11... | collective-permute-start | bytes 4718600 | tf_op jit(solution)/shard_map/ppermute | solution.py:131
  246.2 4.7 %copy-start.2 = (bf16[512,1536]{1,0:T(8,128)(2,1)}, bf16[512,1536]{1,0:T(8,128)(2,1)S(1)}, u32[]{:S(2)}) copy-start(bf16[512,1536]{1,0:T(8,128)(2,1)S(1)} %collective-permute-done.17.refs_6_) | copy-start | bytes 4718596
  247.3 5.5 %copy-start.6 = (bf16[1536,64]{0,1:T(8,128)(2,1)S(1)}, bf16[1536,64]{0,1:T(8,128)(2,1)}, u32[]{:S(2)}) copy-start(bf16[1536,64]{0,1:T(8,128)(2,1)} %param.23) | copy-start | bytes 589828
  247.3 20.7 %collective-permute-start.18 = (bf16[256,1536]{1,0:T(8,128)(2,1)}, bf16[256,1536]{1,0:T(8,128)(2,1)}, u32[]{:S(2)}, u32[]{:S(2)}) collective-permute-start(bf16[256,1536]{1,0:T(8,128)(2,1)} %add_convert_fusion), channel_id=1, source_target_pairs={{0,2},{1,3},{2,0},{3,1},{4,6},{5,7},{6,4},{7,5},{8,10},{9,11},{10,... | collective-permute-start | bytes 2359304 | tf_op jit(solution)/shard_map/ppermute | solution.py:131
  249.7 1.4 copy-start.4
  251.1 33.2 %collective-permute-start.11 = (bf16[256,1536]{1,0:T(8,128)(2,1)}, bf16[256,1536]{1,0:T(8,128)(2,1)}, u32[]{:S(2)}, u32[]{:S(2)}) collective-permute-start(bf16[256,1536]{1,0:T(8,128)(2,1)} %add_convert_fusion.1), channel_id=1, source_target_pairs={{0,2},{1,3},{2,0},{3,1},{4,6},{5,7},{6,4},{7,5},{8,10},{9,11},{10,... | collective-permute-start | bytes 2359304 | tf_op jit(solution)/shard_map/ppermute | solution.py:131
  284.3 9.1 %copy-start.7 = (f32[2,256,32]{1,2,0:T(8,128)S(1)}, f32[2,256,32]{1,2,0:T(8,128)}, u32[]{:S(2)}) copy-start(f32[2,256,32]{1,2,0:T(8,128)} %param.16) | copy-start | bytes 196612
  291.9 5.1 %collective-permute-start.19 = (bf16[2,256,32]{2,1,0:T(8,128)(2,1)S(1)}, bf16[2,256,32]{2,1,0:T(8,128)(2,1)}, u32[]{:S(2)}, u32[]{:S(2)}) collective-permute-start(bf16[2,256,32]{2,1,0:T(8,128)(2,1)S(1)} %dynamic-slice_convert_fusion), channel_id=1, source_target_pairs={{0,16},{16,0},{1,17},{17,1},{2,18},{18,2},{3,19},{19,3},{4,20},{20... | collective-permute-start | bytes 98312 | tf_op jit(solution)/shard_map/ppermute | solution.py:15
Sparse Core Ops, SparseCore 0:
  10.1 81.8 all-gather.3
  94.1 78.3 all-gather.5
